TPU v7x, 32 devices: a whole 2x2x4 slice. The times are simulated.
32 devices in a mesh: dp: 8 (over y, x, core), tensor: 4 (over z).
Axes of the slice: x: 2, y: 2, z: 4, core: 2. Of those that a mesh axis runs over, the one named last changes fastest.
Arguments:
- layer_input: bfloat16 [20480, 2048], P('dp', 'tensor'), may hold values from -6 to 6
- positions: int32 [20480], P('dp'), may hold values from -1 to 2559, as said below
- norm_first: bfloat16 [2048], P('tensor'), may hold values from 0.5 to 1.5
- w_query: bfloat16 [2048, 2048], P(None, 'tensor'), may hold values from -0.125 to 0.125
- w_key: bfloat16 [2048, 256], replicated, may hold values from -0.125 to 0.125
- w_value: bfloat16 [2048, 256], replicated, may hold values from -0.125 to 0.125
- w_out: bfloat16 [2048, 2048], P('tensor'), may hold values from -1.5 to 1.5
- norm_second: bfloat16 [2048], P('tensor'), may hold values from 0.5 to 1.5
- w_gate: bfloat16 [2048, 5632], P(None, 'tensor'), may hold values from -0.125 to 0.125
- w_up: bfloat16 [2048, 5632], P(None, 'tensor'), may hold values from -0.125 to 0.125
- w_down: bfloat16 [5632, 2048], P('tensor'), may hold values from -0.078125 to 0.078125
- cotangent: bfloat16 [20480, 2048], P('dp', 'tensor'), may hold values from -6 to 6
Outputs:
- mixed: bfloat16 [20480, 2048], P('dp', 'tensor')
- grad_input: float32 [20480, 2048], P('dp', 'tensor')
- grad_norm_first: float32 [2048], P(('dp', 'tensor'))
- grad_query: float32 [2048, 2048], P('dp', 'tensor')
- grad_key: float32 [2048, 256], P(('dp', 'tensor'))
- grad_value: float32 [2048, 256], P(('dp', 'tensor'))
- grad_out: float32 [2048, 2048], P('tensor', 'dp')
- grad_norm_second: float32 [2048], P(('dp', 'tensor'))
- grad_gate: float32 [2048, 5632], P('dp', 'tensor')
- grad_up: float32 [2048, 5632], P('dp', 'tensor')
- grad_down: float32 [5632, 2048], P('tensor', 'dp')
Inputs may be any that keep to these rules, and one draw needn't show every extreme that they name: `positions`: each group of 2560 rows holds whole sequences of 1024 or more tokens laid end to end from its first row, numbered 0, 1, 2, ...; its unused rows follow them and hold -1. In every draw one group holds a single sequence of 2560 tokens, another group holds two or more sequences, and every group but the one with the single 2560-token sequence has unused rows.
All inputs are finite; a program needn't handle non-finite values.
Results may differ from a plain program's by a relative error of at most 0.024.
Values may be sent and summed in bfloat16 or wider, within the bound.
A program may use at most 576 MiB of HBM per device.

v0:
```python
import math

import jax
import jax.numpy as jnp
from jax import lax
from jax.sharding import PartitionSpec as P

D = 2048
HD = 64
QBLK = 512


EPS = 1e-05
MASKED = -1e30


def rotate(values, places, direction):
    half_dim = values.shape[-1] // 2
    frequency = 10000.0 ** (-(jnp.arange(half_dim, dtype=jnp.float32) * 2.0 / values.shape[-1]))
    angles = places.astype(jnp.float32)[:, None] * frequency[None, :]
    cosine = jnp.cos(angles)[:, None, :]
    sines = direction * jnp.sin(angles)[:, None, :]
    front_half = values[..., :half_dim]
    back_half = values[..., half_dim:]
    return jnp.concatenate(
        [front_half * cosine - back_half * sines, back_half * cosine + front_half * sines], axis=-1
    )


def visible_rows(first_row, row_count, places, key_count):
    rows_here = first_row + jnp.arange(row_count, dtype=jnp.int32)
    key_index = jnp.arange(key_count, dtype=jnp.int32)
    query_places = places[first_row : first_row + row_count]
    key_places = places[:key_count]
    visible = (key_index[None, :] <= rows_here[:, None]) & (key_places[None, :] >= 0)
    visible = visible & (
        query_places[:, None] - key_places[None, :] == rows_here[:, None] - key_index[None, :]
    )
    return visible | (key_index[None, :] == rows_here[:, None])


def contract_rows(left_side, right_side):
    return lax.dot_general(
        left_side, right_side, (((0,), (0,)), ((), ())), preferred_element_type=jnp.float32
    )


def contract_cols(left_side, right_side):
    return lax.dot_general(
        left_side, right_side, (((1,), (1,)), ((), ())), preferred_element_type=jnp.float32
    )


def local(
    layer_input,
    positions,
    norm_first,
    w_query,
    w_key,
    w_value,
    w_out,
    norm_second,
    w_gate,
    w_up,
    w_down,
    cotangent,
):
    tensor_size = lax.axis_size("tensor")
    tensor_rank = lax.axis_index("tensor")
    capacity = layer_input.shape[0]
    own_width = layer_input.shape[1]
    model_width = w_key.shape[0]
    local_heads = w_query.shape[1] // HD
    kv_share = tensor_size // (w_key.shape[1] // HD)
    kv_head = tensor_rank // kv_share
    score_scale = 1.0 / math.sqrt(HD)
    blocks = capacity // QBLK
    full_rows, gain_one, gain_two = (
        lax.all_gather(layer_input, "tensor", axis=1, tiled=True),
        lax.all_gather(norm_first, "tensor", axis=0, tiled=True),
        lax.all_gather(norm_second, "tensor", axis=0, tiled=True),
    )
    rows_float = full_rows.astype(jnp.float32)
    gain_first = gain_one.astype(jnp.float32)
    gain_second = gain_two.astype(jnp.float32)
    scale_first = lax.rsqrt(jnp.mean(rows_float * rows_float, axis=1, keepdims=True) + EPS)
    normed_first = (rows_float * scale_first * gain_first).astype(jnp.bfloat16)
    key_cols = lax.dynamic_slice_in_dim(w_key, kv_head * HD, HD, 1)
    value_cols = lax.dynamic_slice_in_dim(w_value, kv_head * HD, HD, 1)
    query_lin = jnp.dot(normed_first, w_query, preferred_element_type=jnp.float32)
    queries = rotate(query_lin.reshape(capacity, local_heads, HD), positions, 1.0).astype(
        jnp.bfloat16
    )
    key_lin = jnp.dot(normed_first, key_cols, preferred_element_type=jnp.float32)
    key_rows = (
        rotate(key_lin.reshape(capacity, 1, HD), positions, 1.0)
        .reshape(capacity, HD)
        .astype(jnp.bfloat16)
    )
    value_rows = jnp.dot(normed_first, value_cols, preferred_element_type=jnp.float32).astype(
        jnp.bfloat16
    )
    block_outputs = []
    block_logsums = []
    for block_index in range(blocks):
        first_row = block_index * QBLK
        key_count = first_row + QBLK
        visible = visible_rows(first_row, QBLK, positions, key_count)
        scores = (
            jnp.einsum(
                "qhd,kd->qhk",
                queries[first_row:key_count],
                key_rows[:key_count],
                preferred_element_type=jnp.float32,
            )
            * score_scale
        )
        scores = jnp.where(visible[:, None, :], scores, MASKED)
        row_top = jnp.max(scores, axis=-1, keepdims=True)
        weights = jnp.exp(scores - row_top)
        row_total = jnp.sum(weights, axis=-1, keepdims=True)
        probabilities = (weights / row_total).astype(jnp.bfloat16)
        block_outputs.append(
            jnp.einsum(
                "qhk,kd->qhd",
                probabilities,
                value_rows[:key_count],
                preferred_element_type=jnp.float32,
            )
        )
        block_logsums.append(row_top[..., 0] + jnp.log(row_total[..., 0]))
    attended = (
        jnp.concatenate(block_outputs, axis=0)
        .reshape(capacity, local_heads * HD)
        .astype(jnp.bfloat16)
    )
    log_totals = jnp.concatenate(block_logsums, axis=0)
    attn_part = lax.psum_scatter(
        jnp.dot(attended, w_out, preferred_element_type=jnp.float32).astype(jnp.bfloat16),
        "tensor",
        scatter_dimension=1,
        tiled=True,
    ).astype(jnp.float32)
    own_rows = layer_input.astype(jnp.float32)
    residual = own_rows + attn_part
    mid_full = lax.all_gather(residual.astype(jnp.bfloat16), "tensor", axis=1, tiled=True).astype(
        residual.dtype
    )
    scale_second = lax.rsqrt(jnp.mean(mid_full * mid_full, axis=1, keepdims=True) + EPS)
    normed_second = (mid_full * scale_second * gain_second).astype(jnp.bfloat16)
    gate_act = jnp.dot(normed_second, w_gate, preferred_element_type=jnp.float32)
    upward = jnp.dot(normed_second, w_up, preferred_element_type=jnp.float32)
    sigmoid_gate = jax.nn.sigmoid(gate_act)
    hidden = (gate_act * sigmoid_gate * upward).astype(jnp.bfloat16)
    mlp_part = lax.psum_scatter(
        jnp.dot(hidden, w_down, preferred_element_type=jnp.float32).astype(jnp.bfloat16),
        "tensor",
        scatter_dimension=1,
        tiled=True,
    ).astype(jnp.float32)
    mixed = (residual + mlp_part).astype(jnp.bfloat16)
    grad_rows = lax.all_gather(cotangent, "tensor", axis=1, tiled=True)
    grad_wdown = contract_rows(hidden, grad_rows)
    grad_hidden = contract_cols(grad_rows, w_down)
    grad_gate_act = (
        grad_hidden * upward * sigmoid_gate * (1.0 + gate_act * (1.0 - sigmoid_gate))
    ).astype(jnp.bfloat16)
    grad_upward = (grad_hidden * gate_act * sigmoid_gate).astype(jnp.bfloat16)
    grad_wgate = contract_rows(normed_second, grad_gate_act)
    grad_wup = contract_rows(normed_second, grad_upward)
    grad_normed_second = contract_cols(grad_gate_act, w_gate) + contract_cols(grad_upward, w_up)
    stat_second = jnp.broadcast_to(
        jnp.sum(grad_normed_second * gain_second * mid_full, axis=1, keepdims=True),
        (capacity, tensor_size),
    )
    own_second, own_stat_second = (
        lax.psum_scatter(
            grad_normed_second.astype(jnp.bfloat16), "tensor", scatter_dimension=1, tiled=True
        ).astype(jnp.float32),
        lax.psum_scatter(
            stat_second.astype(jnp.bfloat16), "tensor", scatter_dimension=1, tiled=True
        ).astype(jnp.float32),
    )
    own_gain_two = norm_second.astype(jnp.float32)
    grad_residual = (
        cotangent.astype(jnp.float32)
        + own_gain_two * own_second * scale_second
        - residual * scale_second**3 * own_stat_second / D
    )
    gain_two_grad = jnp.sum(own_second * residual * scale_second, axis=0)
    attn_rows = lax.all_gather(grad_residual.astype(jnp.bfloat16), "tensor", axis=1, tiled=True)
    grad_wout = contract_rows(attended, attn_rows)
    grad_attended = (
        contract_cols(attn_rows, w_out).astype(jnp.bfloat16).reshape(capacity, local_heads, HD)
    )
    grad_query_blocks = []
    grad_keys = jnp.zeros((capacity, HD), jnp.float32)
    grad_values = jnp.zeros((capacity, HD), jnp.float32)
    for block_index in range(blocks):
        first_row = block_index * QBLK
        key_count = first_row + QBLK
        visible = visible_rows(first_row, QBLK, positions, key_count)
        block_queries = queries[first_row:key_count]
        scores = (
            jnp.einsum(
                "qhd,kd->qhk",
                block_queries,
                key_rows[:key_count],
                preferred_element_type=jnp.float32,
            )
            * score_scale
        )
        scores = jnp.where(visible[:, None, :], scores, MASKED)
        probabilities = jnp.exp(scores - log_totals[first_row:key_count][..., None])
        probs_low = probabilities.astype(jnp.bfloat16)
        grad_block = grad_attended[first_row:key_count]
        grad_probs = jnp.einsum(
            "qhd,kd->qhk", grad_block, value_rows[:key_count], preferred_element_type=jnp.float32
        )
        row_dot = jnp.sum(grad_probs * probabilities, axis=-1, keepdims=True)
        grad_scores = (probabilities * (grad_probs - row_dot)).astype(jnp.bfloat16)
        grad_query_blocks.append(
            jnp.einsum(
                "qhk,kd->qhd", grad_scores, key_rows[:key_count], preferred_element_type=jnp.float32
            )
            * score_scale
        )
        grad_keys = grad_keys.at[:key_count].add(
            jnp.einsum(
                "qhk,qhd->kd", grad_scores, block_queries, preferred_element_type=jnp.float32
            )
            * score_scale
        )
        grad_values = grad_values.at[:key_count].add(
            jnp.einsum("qhk,qhd->kd", probs_low, grad_block, preferred_element_type=jnp.float32)
        )
    grad_query_rot = jnp.concatenate(grad_query_blocks, axis=0)
    grad_query_lin = (
        rotate(grad_query_rot, positions, -1.0)
        .reshape(capacity, local_heads * HD)
        .astype(jnp.bfloat16)
    )
    grad_key_lin = (
        rotate(grad_keys.reshape(capacity, 1, HD), positions, -1.0)
        .reshape(capacity, HD)
        .astype(jnp.bfloat16)
    )
    grad_value_lin = grad_values.astype(jnp.bfloat16)
    grad_wquery = contract_rows(normed_first, grad_query_lin)
    grad_wkey_head = contract_rows(normed_first, grad_key_lin)
    grad_wvalue_head = contract_rows(normed_first, grad_value_lin)
    grad_normed_first = (
        contract_cols(grad_query_lin, w_query)
        + contract_cols(grad_key_lin, key_cols)
        + contract_cols(grad_value_lin, value_cols)
    )
    stat_first = jnp.broadcast_to(
        jnp.sum(grad_normed_first * gain_first * rows_float, axis=1, keepdims=True),
        (capacity, tensor_size),
    )
    own_first, own_stat_first = (
        lax.psum_scatter(
            grad_normed_first.astype(jnp.bfloat16), "tensor", scatter_dimension=1, tiled=True
        ).astype(jnp.float32),
        lax.psum_scatter(
            stat_first.astype(jnp.bfloat16), "tensor", scatter_dimension=1, tiled=True
        ).astype(jnp.float32),
    )
    own_gain_one = norm_first.astype(jnp.float32)
    grad_input = (
        grad_residual
        + own_gain_one * own_first * scale_first
        - own_rows * scale_first**3 * own_stat_first / D
    )
    gain_one_grad = jnp.sum(own_first * own_rows * scale_first, axis=0)
    query_out, gate_out, up_out = (
        lax.psum_scatter(
            grad_wquery.astype(jnp.bfloat16), "dp", scatter_dimension=0, tiled=True
        ).astype(jnp.float32),
        lax.psum_scatter(
            grad_wgate.astype(jnp.bfloat16), "dp", scatter_dimension=0, tiled=True
        ).astype(jnp.float32),
        lax.psum_scatter(
            grad_wup.astype(jnp.bfloat16), "dp", scatter_dimension=0, tiled=True
        ).astype(jnp.float32),
    )
    wout_out, down_out = (
        lax.psum_scatter(
            grad_wout.astype(jnp.bfloat16), "dp", scatter_dimension=1, tiled=True
        ).astype(jnp.float32),
        lax.psum_scatter(
            grad_wdown.astype(jnp.bfloat16), "dp", scatter_dimension=1, tiled=True
        ).astype(jnp.float32),
    )
    key_full = lax.dynamic_update_slice_in_dim(
        jnp.zeros((model_width, w_key.shape[1]), jnp.float32), grad_wkey_head, kv_head * HD, 1
    )
    value_full = lax.dynamic_update_slice_in_dim(
        jnp.zeros((model_width, w_value.shape[1]), jnp.float32), grad_wvalue_head, kv_head * HD, 1
    )
    gain_one_full = lax.dynamic_update_slice_in_dim(
        jnp.zeros((model_width,), jnp.float32), gain_one_grad, tensor_rank * own_width, 0
    )
    gain_two_full = lax.dynamic_update_slice_in_dim(
        jnp.zeros((model_width,), jnp.float32), gain_two_grad, tensor_rank * own_width, 0
    )
    key_out, value_out, gain_one_out, gain_two_out = (
        lax.psum_scatter(key_full, ("dp", "tensor"), scatter_dimension=0, tiled=True),
        lax.psum_scatter(value_full, ("dp", "tensor"), scatter_dimension=0, tiled=True),
        lax.psum_scatter(gain_one_full, ("dp", "tensor"), scatter_dimension=0, tiled=True),
        lax.psum_scatter(gain_two_full, ("dp", "tensor"), scatter_dimension=0, tiled=True),
    )
    return (
        mixed,
        grad_input,
        gain_one_out,
        query_out,
        key_out,
        value_out,
        wout_out,
        gain_two_out,
        gate_out,
        up_out,
        down_out,
    )


def solution(mesh):
    return jax.shard_map(
        local,
        mesh=mesh,
        in_specs=(
            P("dp", "tensor"),
            P("dp"),
            P("tensor"),
            P(None, "tensor"),
            P(),
            P(),
            P("tensor", None),
            P("tensor"),
            P(None, "tensor"),
            P(None, "tensor"),
            P("tensor", None),
            P("dp", "tensor"),
        ),
        out_specs=(
            P("dp", "tensor"),
            P("dp", "tensor"),
            P(("dp", "tensor")),
            P("dp", "tensor"),
            P(("dp", "tensor"), None),
            P(("dp", "tensor"), None),
            P("tensor", "dp"),
            P(("dp", "tensor")),
            P("dp", "tensor"),
            P("dp", "tensor"),
            P("tensor", "dp"),
        ),
        check_vma=False,
    )
```

profile of v0, /device:TPU:0, one launch (start us, length us, event | category | flops | bytes accessed | tf_op | source)
XLA Modules:
  0.0 2357.7 jit_solution(9880270018765540656)
XLA Ops:
  44.6 151.7 %all-gather.7.cloned.1.call-done = bf16[2560,2048]{1,0:T(8,128)(2,1)} async-done(((bf16[2560,512]{1,0:T(8,128)(2,1)}), bf16[2560,2048]{1,0:T(8,128)(2,1)}) %all-gather.7.cloned.1.call-update) | async-done | bytes 10485776 | tf_op jit(solution)/shard_map/all_gather | solution.py:79
  398.0 176.3 %reduce-scatter.12.cloned.1.call-done = bf16[2560,512]{1,0:T(8,128)(2,1)} async-done(((bf16[2560,2048]{1,0:T(8,128)(2,1)}), bf16[2560,512]{1,0:T(8,128)(2,1)}) %reduce-scatter.12.cloned.1.call-update) | async-done | bytes 2621456 | tf_op jit(solution)/shard_map/reduce_scatter | solution.py:138
  592.9 171.3 %all-gather.9.cloned.1.call-done = bf16[2560,2048]{1,0:T(8,128)(2,1)} async-done(((bf16[2560,512]{1,0:T(8,128)(2,1)}), bf16[2560,2048]{1,0:T(8,128)(2,1)}) %all-gather.9.cloned.1.call-update) | async-done | bytes 10485776 | tf_op jit(solution)/shard_map/all_gather | solution.py:146
  771.6 21.0 fusion.207
  813.3 134.5 %all-gather.11.cloned.1.call-done = bf16[2560,2048]{1,0:T(8,128)(2,1)} async-done(((bf16[2560,512]{1,0:T(8,128)(2,1)}), bf16[2560,2048]{1,0:T(8,128)(2,1)}) %all-gather.11.cloned.1.call-update) | async-done | bytes 10485776 | tf_op jit(solution)/shard_map/all_gather | solution.py:162
  947.7 31.4 %multiply_convert_fusion.4 = (bf16[2560,1408]{1,0:T(8,128)(2,1)}, bf16[2560,1408]{1,0:T(8,128)(2,1)}, bf16[2560,1408]{1,0:T(8,128)(2,1)}) fusion(f32[2560,1408]{1,0:T(8,128)} %fusion.209, f32[2560,1408]{1,0:T(8,128)} %fusion.207, bf16[2560,2048]{1,0:T(8,128)(2,1)} %all-gather.11.cloned.1.call-done, bf16[1408,2048]{1,0:T(8,128)(2,1)} %param.46), kind=kOutput, calls=%fused_computation.52 | convolution fusion | flops 14821621760 | bytes 66715648 | tf_op jit(solution)/shard_map/dot_general | solution.py:49
  979.1 22.6 fusion.220
  1001.7 25.9 %fusion.211 = (bf16[2560,2048]{1,0:T(8,128)(2,1)}, bf16[2560]{0:T(1024)(128)(2,1)S(1)}) fusion(bf16[2560,2048]{1,0:T(8,128)(2,1)} %all-gather.9.cloned.1.call-done, f32[2048]{0:T(1024)S(1)} %bitcast.232, f32[2560,2048]{1,0:T(8,128)} %fusion.220, bf16[2560,1408]{1,0:T(8,128)(2,1)} %get-tuple-element.151, bf16[2048,1408]{1,0:T(8,128)(2,1)} %param.45), kind=kOutput, calls=%fused_computation.296 | convolution fusion | flops 14795405312 | bytes 54932480 | tf_op jit(solution)/shard_map/dot_general | solution.py:49
  1046.3 158.7 %reduce-scatter.16.cloned.1.call-done = bf16[2560,512]{1,0:T(8,128)(2,1)} async-done(((bf16[2560,2048]{1,0:T(8,128)(2,1)}), bf16[2560,512]{1,0:T(8,128)(2,1)}) %reduce-scatter.16.cloned.1.call-update) | async-done | bytes 2621456 | tf_op jit(solution)/shard_map/reduce_scatter | solution.py:177
  1211.2 21.2 convolution_convert_fusion.2
  1232.5 23.1 convolution_convert_fusion.3
  1255.8 23.0 convolution_convert_fusion.4
  1279.1 117.0 %all-gather.13.cloned.1.call-done = bf16[2560,2048]{1,0:T(8,128)(2,1)} async-done(((bf16[2560,512]{1,0:T(8,128)(2,1)}), bf16[2560,2048]{1,0:T(8,128)(2,1)}) %all-gather.13.cloned.1.call-update) | async-done | bytes 10485776 | tf_op jit(solution)/shard_map/all_gather | solution.py:191
  1464.1 21.2 multiply_reduce_fusion.2
  1511.6 23.7 %multiply_reduce_fusion.1 = (f32[512,8]{0,1:T(8,128)S(1)}, f32[512,8,2048]{2,0,1:T(8,128)}) fusion(f32[512,8,2048]{2,0,1:T(8,128)} %get-tuple-element.192, f32[512,8]{0,1:T(8,128)S(1)} %log_add_fusion.1, bf16[512,8,64]{0,2,1:T(8,128)(2,1)S(1)} %bitcast.217, bf16[2560,64]{0,1:T(8,128)(2,1)S(1)} %copy-done.24), kind=kOutput, calls=%fused_computation.8 | convolution fusion | flops 1098903552 | bytes 67928064 | tf_op jit(solution)/shard_map/qhd,kd->qhk/dot_general | solution.py:217
  1535.3 29.7 %multiply_convert_fusion.1 = bf16[512,8,2048]{2,0,1:T(8,128)(2,1)} fusion(f32[512,8,2048]{2,0,1:T(8,128)} %get-tuple-element.202, f32[512,8,2048]{2,0,1:T(8,128)} %get-tuple-element.192, f32[512,8]{0,1:T(8,128)S(1)} %get-tuple-element.201, f32[512,8]{0,1:T(8,128)S(1)} %log_add_fusion.1), kind=kLoop, calls=%fused_computation.7 | loop fusion | flops 33554432 | bytes 83918848 | tf_op jit(solution)/shard_map/convert_element_type | solution.py:221
  1577.0 27.9 %multiply_reduce_fusion = (f32[512,8]{0,1:T(8,128)S(1)}, f32[512,8,2560]{2,0,1:T(8,128)}) fusion(f32[512,8,2560]{2,0,1:T(8,128)} %get-tuple-element.194, f32[512,8]{0,1:T(8,128)S(1)} %log_add_fusion, bf16[512,8,64]{0,2,1:T(8,128)(2,1)S(1)} %bitcast.215, bf16[2560,64]{0,1:T(8,128)(2,1)S(1)} %copy-done.24), kind=kOutput, calls=%fused_computation.1 | convolution fusion | flops 1373630464 | bytes 84770816 | tf_op jit(solution)/shard_map/qhd,kd->qhk/dot_general | solution.py:217
  1604.9 34.6 %multiply_convert_fusion = bf16[512,8,2560]{2,0,1:T(8,128)(2,1)} fusion(f32[512,8,2560]{2,0,1:T(8,128)} %get-tuple-element.204, f32[512,8,2560]{2,0,1:T(8,128)} %get-tuple-element.194, f32[512,8]{0,1:T(8,128)S(1)} %get-tuple-element.203, f32[512,8]{0,1:T(8,128)S(1)} %log_add_fusion), kind=kLoop, calls=%fused_computation | loop fusion | flops 41943040 | bytes 104890368 | tf_op jit(solution)/shard_map/convert_element_type | solution.py:221
  1667.1 22.0 convolution_convert_fusion
  1792.2 22.9 fusion.8
  1888.4 181.5 %reduce-scatter.18.cloned.1.call-done = bf16[2560,512]{1,0:T(8,128)(2,1)} async-done(((bf16[2560,2048]{1,0:T(8,128)(2,1)}), bf16[2560,512]{1,0:T(8,128)(2,1)}) %reduce-scatter.18.cloned.1.call-update) | async-done | bytes 2621456 | tf_op jit(solution)/shard_map/reduce_scatter | solution.py:262
  2082.5 41.5 %all-reduce.6 = (f32[2048]{0:T(1024)S(1)}, f32[2048]{0:T(1024)S(1)}) all-reduce(f32[2048]{0:T(1024)S(1)} %dynamic_update_slice.12, f32[2048]{0:T(1024)S(1)} %dynamic_update_slice.15), channel_id=8, replica_groups=mesh['dp'=8,'tensor'=4] {'dp','tensor'}, use_global_device_ids=true, to_apply=%region_26.27.clone | all-reduce | flops 4096 | bytes 32768
  2125.2 87.1 %reduce-scatter.24.cloned.1.call-done = f32[64,256]{1,0:T(8,128)} async-done(((f32[2048,256]{1,0:T(8,128)}), f32[64,256]{1,0:T(8,128)}) %reduce-scatter.24.cloned.1.call-update) | async-done | bytes 65552 | tf_op jit(solution)/shard_map/reduce_scatter | solution.py:309
  2212.3 138.8 %reduce-scatter.22.cloned.1.call-done = f32[64,256]{1,0:T(8,128)} async-done(((f32[2048,256]{1,0:T(8,128)}), f32[64,256]{1,0:T(8,128)}) %reduce-scatter.22.cloned.1.call-update) | async-done | bytes 65552 | tf_op jit(solution)/shard_map/reduce_scatter | solution.py:308
  (408 shorter events, 633.6 us)
Async XLA Ops:
  7.2 380.8 %copy-start = (bf16[512,2048]{1,0:T(8,128)(2,1)S(1)}, bf16[512,2048]{1,0:T(8,128)(2,1)}, u32[]{:S(2)}) copy-start(bf16[512,2048]{1,0:T(8,128)(2,1)} %param.42) | copy-start | bytes 6291460
  7.2 189.1 %all-gather.7.cloned.1.call-start = ((), (), s32[]{:S(2)}) async-start(), calls=%async_computation.11 | async-start | bytes 13107200 | tf_op jit(solution)/shard_map/all_gather | solution.py:79
  7.9 566.3 %reduce-scatter.12.cloned.1.call-start = ((), (), s32[]{:S(2)}) async-start(), calls=%async_computation.12 | async-start | bytes 13107200 | tf_op jit(solution)/shard_map/reduce_scatter | solution.py:138
  397.9 366.3 %all-gather.9.cloned.1.call-start = ((), (), s32[]{:S(2)}) async-start(), calls=%async_computation.13 | async-start | bytes 13107200 | tf_op jit(solution)/shard_map/all_gather | solution.py:146
  579.0 368.7 %all-gather.11.cloned.1.call-start = ((), (), s32[]{:S(2)}) async-start(), calls=%async_computation.15 | async-start | bytes 13107200 | tf_op jit(solution)/shard_map/all_gather | solution.py:162
  579.6 625.3 %reduce-scatter.16.cloned.1.call-start = ((), (), s32[]{:S(2)}) async-start(), calls=%async_computation.16 | async-start | bytes 13107200 | tf_op jit(solution)/shard_map/reduce_scatter | solution.py:177
  771.0 484.8 %copy-start.67 = (f32[2560]{0:T(1024)}, f32[2560]{0:T(1024)S(1)}, u32[]{:S(2)}) copy-start(f32[2560]{0:T(1024)S(1)} %get-tuple-element.179) | copy-start | bytes 30724
  1027.7 368.4 %all-gather.13.cloned.1.call-start = ((), (), s32[]{:S(2)}) async-start(), calls=%async_computation.17 | async-start | bytes 13107200 | tf_op jit(solution)/shard_map/all_gather | solution.py:191
  1211.2 633.0 %reduce-scatter.32.cloned.1.call-start = ((), (), s32[]{:S(2)}) async-start(), calls=%async_computation.25 | async-start | bytes 6488064 | tf_op jit(solution)/shard_map/reduce_scatter | solution.py:291
  1232.5 614.0 %reduce-scatter.30.cloned.1.call-start = ((), (), s32[]{:S(2)}) async-start(), calls=%async_computation.24 | async-start | bytes 6488064 | tf_op jit(solution)/shard_map/reduce_scatter | solution.py:283
  1255.7 593.0 %reduce-scatter.28.cloned.1.call-start = ((), (), s32[]{:S(2)}) async-start(), calls=%async_computation.23 | async-start | bytes 6488064 | tf_op jit(solution)/shard_map/reduce_scatter | solution.py:280
  1278.8 592.9 %reduce-scatter.26.cloned.1.call-start = ((), (), s32[]{:S(2)}) async-start(), calls=%async_computation.22 | async-start | bytes 2359296 | tf_op jit(solution)/shard_map/reduce_scatter | solution.py:288
  1279.1 256.2 %copy-start.34 = (f32[512,8]{0,1:T(8,128)}, f32[512,8]{0,1:T(8,128)S(1)}, u32[]{:S(2)}) copy-start(f32[512,8]{0,1:T(8,128)S(1)} %log_add_fusion.1) | copy-start | bytes 49156
  1432.3 441.2 %reduce-scatter.20.cloned.1.call-start = ((), (), s32[]{:S(2)}) async-start(), calls=%async_computation.19 | async-start | bytes 2359296 | tf_op jit(solution)/shard_map/reduce_scatter | solution.py:277
  1667.1 221.4 %reduce-scatter.14.cloned.1.call-start = ((), (), s32[]{:S(2)}) async-start(), calls=%async_computation.14 | async-start | bytes 13107200 | tf_op jit(solution)/shard_map/reduce_scatter | solution.py:155
  1689.1 380.8 %reduce-scatter.18.cloned.1.call-start = ((), (), s32[]{:S(2)}) async-start(), calls=%async_computation.18 | async-start | bytes 13107200 | tf_op jit(solution)/shard_map/reduce_scatter | solution.py:262
  1815.1 397.2 %reduce-scatter.24.cloned.1.call-start = ((), (), s32[]{:S(2)}) async-start(), calls=%async_computation.21 | async-start | bytes 2162688 | tf_op jit(solution)/shard_map/reduce_scatter | solution.py:309
  1830.9 520.2 %reduce-scatter.22.cloned.1.call-start = ((), (), s32[]{:S(2)}) async-start(), calls=%async_computation.20 | async-start | bytes 2162688 | tf_op jit(solution)/shard_map/reduce_scatter | solution.py:308
  1836.7 233.2 %copy-start.62 = (f32[2560]{0:T(1024)S(1)}, f32[2560]{0:T(1024)}, u32[]{:S(2)}) copy-start(f32[2560]{0:T(1024)} %copy-done.61) | copy-start | bytes 30724
  1836.7 233.2 %copy-start.64 = (f32[2560]{0:T(1024)S(1)}, f32[2560]{0:T(1024)}, u32[]{:S(2)}) copy-start(f32[2560]{0:T(1024)} %copy-done.63) | copy-start | bytes 30724
  1836.7 233.2 %copy-start.66 = (f32[2560]{0:T(1024)S(1)}, f32[2560]{0:T(1024)}, u32[]{:S(2)}) copy-start(f32[2560]{0:T(1024)} %get-tuple-element.178) | copy-start | bytes 30724
  1836.7 233.2 %copy-start.68 = (f32[2560]{0:T(1024)S(1)}, f32[2560]{0:T(1024)}, u32[]{:S(2)}) copy-start(f32[2560]{0:T(1024)} %copy-done.67) | copy-start | bytes 30724
  1836.8 233.2 %copy-start.83 = (f32[2560]{0:T(1024)S(1)}, f32[2560]{0:T(1024)}, u32[]{:S(2)}) copy-start(f32[2560]{0:T(1024)} %get-tuple-element.176) | copy-start | bytes 30724
  1836.8 233.2 %copy-start.85 = (f32[512]{0:T(512)S(1)}, f32[512]{0:T(512)}, u32[]{:S(2)}) copy-start(f32[512]{0:T(512)} %copy-done.84) | copy-start | bytes 6148
  (114 other events, 3634.5 us)
Sparse Core Ops, SparseCore 0:
  9.6 186.6 all-gather.6
  398.0 176.1 reduce-scatter.11
  579.2 184.9 all-gather.8
  765.6 182.0 all-gather.10
  1027.9 177.0 reduce-scatter.15
  1211.3 184.7 all-gather.12
  1399.5 57.2 reduce-scatter.31
  1460.7 59.0 reduce-scatter.29
  1523.2 58.9 reduce-scatter.27
  1585.7 41.2 reduce-scatter.25
  1667.2 39.7 reduce-scatter.19
  1709.4 179.0 reduce-scatter.13
  1890.9 179.0 reduce-scatter.17
  2072.7 139.4 reduce-scatter.23
  2215.0 136.0 reduce-scatter.21
where the time goes:
time: 2360 us
  waiting for transfers between devices  1330 us (56%)
  matrix products  638 us (27%)
  other arithmetic  220 us (9%)
  blocking collectives  105 us (4%)
  local copies, waits for them, and re-layouts  47 us (2%)
    reduce_scatter x1, waiting for transfers between devices, local(): lax.psum_scatter(grad_normed_first.astype(jnp.bfloat16), 'tensor', scatte...  182 us
    reduce_scatter x1, waiting for transfers between devices, local(): lax.psum_scatter(jnp.dot(attended, w_out, preferred_element_type=jnp.floa...  176 us
    all_gather x1, waiting for transfers between devices, local(): lax.all_gather(residual.astype(jnp.bfloat16), 'tensor', axis=1, tiled=True)  171 us
    reduce_scatter x1, waiting for transfers between devices, local(): lax.psum_scatter(grad_normed_second.astype(jnp.bfloat16), 'tensor', scatt...  159 us
    all_gather x1, waiting for transfers between devices, local(): lax.all_gather(layer_input, 'tensor', axis=1, tiled=True)  152 us
    reduce_scatter x1, waiting for transfers between devices, local(): lax.psum_scatter(key_full, ('dp', 'tensor'), scatter_dimension=0, tiled=T...  139 us
    all_gather x1, waiting for transfers between devices, local(): grad_rows = lax.all_gather(cotangent, 'tensor', axis=1, tiled=True)  134 us
    dot_general x7, matrix products, contract_cols(): lax.dot_general(left_side, right_side, (((1,), (1,)), ((), ())), preferre...  130 us
  transfers between devices with their start and end apart: 15, of which 10 were waited for; matrix products, arithmetic and copies ran while one was open for 25% of the time, Pallas kernels for 0%

commit v1 on v0

v1 whole, which is shorter than its diff:
```python
import functools

import jax
import jax.numpy as jnp
from jax import lax
from jax.experimental import pallas as pl
from jax.experimental.pallas import tpu as pltpu
from jax.sharding import PartitionSpec as P

HD = 64
EPS = 1e-05
MASKED = -1e30
NB = 5
KC = 256
SUM_ROWS = 16
F32 = jnp.float32
BF16 = jnp.bfloat16


def mm(left, right, dims):
    return lax.dot_general(left, right, ((dims[0], dims[1]), ((), ())), preferred_element_type=F32)


def spans(bounds_ref, r):
    return tuple(bounds_ref[r, i] for i in range(4))


def forward_kernel(bounds_ref, q_ref, lo_ref, hi_ref, k_ref, vt_ref, o_ref, lse_ref, acc_ref, top_ref):
    r = pl.program_id(1)
    share = q_ref.shape[1] // HD
    width = q_ref.shape[2]
    pairs = share // 2
    first, full_first, full_last, last = spans(bounds_ref, r)
    low = lo_ref[0]
    high = hi_ref[0]
    low2 = jnp.concatenate([low, low], axis=1)
    high2 = jnp.concatenate([high, high], axis=1)
    acc_ref[...] = jnp.zeros_like(acc_ref)
    top_ref[...] = jnp.full_like(top_ref, MASKED)

    def chunk(c, masked):
        keys = k_ref[0, pl.ds(pl.multiple_of(c * KC, KC), KC), :]
        values_t = vt_ref[0, c]
        if masked:
            index = lax.broadcasted_iota(jnp.int32, (KC, 2 * width), 0) + c * KC
            visible = (index >= low2) & (index <= high2)
        for p in range(pairs):
            queries = jnp.concatenate(
                [q_ref[0, (2 * p) * HD : (2 * p + 1) * HD, :], q_ref[0, (2 * p + 1) * HD : (2 * p + 2) * HD, :]], axis=1
            )
            scores = mm(keys, queries, ((1,), (0,)))
            if masked:
                scores = jnp.where(visible, scores, MASKED)
            old = top_ref[p]
            top = jnp.maximum(old, jnp.max(scores, axis=0, keepdims=True))
            weights = jnp.exp(scores - top).astype(BF16)
            top_ref[p] = top
            acc_ref[p] = acc_ref[p] * jnp.exp(old - top) + mm(values_t, weights, ((1,), (0,)))

    @pl.loop(full_first, full_last)
    def _(c):
        chunk(c, False)

    @pl.loop(0, (full_first - first) + (last - full_last))
    def _(t):
        before = full_first - first
        chunk(jnp.where(t < before, first + t, full_last + t - before), True)

    for p in range(pairs):
        acc = acc_ref[p]
        total = acc[HD : HD + 1, :]
        out = acc[:HD, :] / total
        logs = top_ref[p] + jnp.log(total)
        for side in range(2):
            h = 2 * p + side
            cols = slice(side * width, (side + 1) * width)
            o_ref[0, h * HD : (h + 1) * HD, :] = out[:, cols].astype(BF16)
            lse_ref[0, 0, h : h + 1, :] = logs[:, cols]


def backward_kernel(
    bounds_ref, q_ref, do_ref, o_ref, lse_ref, lo_ref, hi_ref, k_ref, v_ref, kt_ref, dq_ref, dk_ref, dv_ref, acc_ref
):
    r = pl.program_id(1)
    share = q_ref.shape[1] // HD
    width = q_ref.shape[2]
    pairs = share // 2
    first, full_first, full_last, last = spans(bounds_ref, r)
    low = lo_ref[0]
    high = hi_ref[0]
    low2 = jnp.concatenate([low, low], axis=1)
    high2 = jnp.concatenate([high, high], axis=1)

    @pl.when(r == 0)
    def _():
        dk_ref[...] = jnp.zeros_like(dk_ref)
        dv_ref[...] = jnp.zeros_like(dv_ref)

    acc_ref[...] = jnp.zeros_like(acc_ref)

    def both(ref, p):
        return jnp.concatenate(
            [ref[0, (2 * p) * HD : (2 * p + 1) * HD, :], ref[0, (2 * p + 1) * HD : (2 * p + 2) * HD, :]], axis=1
        )

    stats = []
    for p in range(pairs):
        logs = jnp.concatenate([lse_ref[0, 0, 2 * p : 2 * p + 1, :], lse_ref[0, 0, 2 * p + 1 : 2 * p + 2, :]], axis=1)
        delta = jnp.sum(both(do_ref, p).astype(F32) * both(o_ref, p).astype(F32), axis=0, keepdims=True)
        stats.append((logs, delta))

    def chunk(c, masked):
        rows = pl.ds(pl.multiple_of(c * KC, KC), KC)
        keys = k_ref[0, rows, :]
        values = v_ref[0, rows, :]
        keys_t = kt_ref[0, c]
        if masked:
            index = lax.broadcasted_iota(jnp.int32, (KC, 2 * width), 0) + c * KC
            visible = (index >= low2) & (index <= high2)
        sum_k = jnp.zeros((KC, HD), F32)
        sum_v = jnp.zeros((KC, HD), F32)
        for p in range(pairs):
            queries = both(q_ref, p)
            douts = both(do_ref, p)
            logs, delta = stats[p]
            probs = jnp.exp(mm(keys, queries, ((1,), (0,))) - logs)
            if masked:
                probs = jnp.where(visible, probs, 0.0)
            dprobs = mm(values, douts, ((1,), (0,)))
            dscores = (probs * (dprobs - delta)).astype(BF16)
            sum_v = sum_v + mm(probs.astype(BF16), douts, ((1,), (1,)))
            sum_k = sum_k + mm(dscores, queries, ((1,), (1,)))
            acc_ref[p] += mm(keys_t, dscores, ((1,), (0,)))
        dk_ref[0, rows, :] += sum_k
        dv_ref[0, rows, :] += sum_v

    @pl.loop(full_first, full_last)
    def _(c):
        chunk(c, False)

    @pl.loop(0, (full_first - first) + (last - full_last))
    def _(t):
        before = full_first - first
        chunk(jnp.where(t < before, first + t, full_last + t - before), True)

    for p in range(pairs):
        for side in range(2):
            h = 2 * p + side
            dq_ref[0, h * HD : (h + 1) * HD, :] = acc_ref[p, :, side * width : (side + 1) * width]


def attend(bounds, q_t, lows, highs, keys, values_t):
    kv, capacity = keys.shape[0], keys.shape[1]
    blocks, wide, width = q_t.shape
    slab = wide // kv
    share = slab // HD
    work = kv * share * blocks * width * capacity // 2
    return pl.pallas_call(
        forward_kernel,
        out_shape=(
            jax.ShapeDtypeStruct((blocks, wide, width), BF16),
            jax.ShapeDtypeStruct((blocks, kv, share, width), F32),
        ),
        grid_spec=pltpu.PrefetchScalarGridSpec(
            num_scalar_prefetch=1,
            grid=(kv, blocks),
            in_specs=[
                pl.BlockSpec((1, slab, width), lambda m, r, b: (r, m, 0)),
                pl.BlockSpec((1, 1, width), lambda m, r, b: (r, 0, 0)),
                pl.BlockSpec((1, 1, width), lambda m, r, b: (r, 0, 0)),
                pl.BlockSpec((1, capacity, HD), lambda m, r, b: (m, 0, 0)),
                pl.BlockSpec((1, capacity // KC, HD + SUM_ROWS, KC), lambda m, r, b: (m, 0, 0, 0)),
            ],
            out_specs=[
                pl.BlockSpec((1, slab, width), lambda m, r, b: (r, m, 0)),
                pl.BlockSpec((1, 1, share, width), lambda m, r, b: (r, m, 0, 0)),
            ],
            scratch_shapes=[
                pltpu.VMEM((share // 2, HD + SUM_ROWS, 2 * width), F32),
                pltpu.VMEM((share // 2, 1, 2 * width), F32),
            ],
        ),
        compiler_params=pltpu.CompilerParams(vmem_limit_bytes=32 * 1024 * 1024),
        cost_estimate=pl.CostEstimate(flops=4 * work * HD * 4, bytes_accessed=12 * 1024 * 1024, transcendentals=work),
        name="attention_forward",
    )(bounds, q_t, lows, highs, keys, values_t)


def attend_back(bounds, q_t, do_t, o_t, lse, lows, highs, keys, values, keys_t):
    kv, capacity = keys.shape[0], keys.shape[1]
    blocks, wide, width = q_t.shape
    slab = wide // kv
    share = slab // HD
    work = kv * share * blocks * width * capacity // 2
    slab_spec = pl.BlockSpec((1, slab, width), lambda m, r, b: (r, m, 0))
    row_spec = pl.BlockSpec((1, 1, width), lambda m, r, b: (r, 0, 0))
    key_spec = pl.BlockSpec((1, capacity, HD), lambda m, r, b: (m, 0, 0))
    return pl.pallas_call(
        backward_kernel,
        out_shape=(
            jax.ShapeDtypeStruct((blocks, wide, width), F32),
            jax.ShapeDtypeStruct((kv, capacity, HD), F32),
            jax.ShapeDtypeStruct((kv, capacity, HD), F32),
        ),
        grid_spec=pltpu.PrefetchScalarGridSpec(
            num_scalar_prefetch=1,
            grid=(kv, blocks),
            in_specs=[
                slab_spec,
                slab_spec,
                slab_spec,
                pl.BlockSpec((1, 1, share, width), lambda m, r, b: (r, m, 0, 0)),
                row_spec,
                row_spec,
                key_spec,
                key_spec,
                pl.BlockSpec((1, capacity // KC, HD, KC), lambda m, r, b: (m, 0, 0, 0)),
            ],
            out_specs=[slab_spec, key_spec, key_spec],
            scratch_shapes=[pltpu.VMEM((share // 2, HD, 2 * width), F32)],
        ),
        compiler_params=pltpu.CompilerParams(vmem_limit_bytes=32 * 1024 * 1024),
        cost_estimate=pl.CostEstimate(flops=10 * work * HD * 4, bytes_accessed=24 * 1024 * 1024, transcendentals=work),
        name="attention_backward",
    )(bounds, q_t, do_t, o_t, lse, lows, highs, keys, values, keys_t)


def shift(array, size, step):
    return lax.ppermute(array, "tensor", [(i, (i + step) % size) for i in range(size)])


def swap(array, size, bit):
    return lax.ppermute(array, "dp", [(i, i ^ (1 << bit)) for i in range(size)])


def pick(stack, index):
    return lax.dynamic_index_in_dim(stack, index, 0, keepdims=False)


def by_owner(array, size):
    width = array.shape[0] // (NB * size)
    grid = array.reshape(NB, size, width, array.shape[1])
    turned = jnp.stack([grid[r] if r % 2 == 0 else grid[r, ::-1] for r in range(NB)], axis=1)
    return turned.reshape(size, NB * width, array.shape[1])


def by_place(stack):
    size, rows, features = stack.shape
    grid = stack.reshape(size, NB, rows // NB, features)
    turned = jnp.stack([grid[:, r] if r % 2 == 0 else grid[::-1, r] for r in range(NB)], axis=0)
    return turned.reshape(size * rows, features)


def exchange(stack, rank):
    size = stack.shape[0]
    parts = [pick(stack, rank)]
    for step in range(1, size):
        parts.append(shift(pick(stack, lax.rem(rank + step, size)), size, step))
    ahead = [parts[(size - j) % size] for j in range(size)]
    both = jnp.stack(ahead + ahead[: size - 1], axis=0)
    return lax.dynamic_slice_in_dim(both, lax.rem(size - rank, size), size, 0)


def to_rows(array, size, rank):
    got = exchange(by_owner(array, size), rank)
    return got.transpose(1, 0, 2).reshape(got.shape[1], -1)


def to_features(array, size, rank):
    rows = array.shape[0]
    stack = array.reshape(rows, size, -1).transpose(1, 0, 2)
    return by_place(exchange(stack, rank))


def gather_shards(shard, dim, dp_size, dp_rank, size):
    length = shard.shape[dim] // dp_size
    piece = lax.dynamic_slice_in_dim(shard, dp_rank * length, length, dim)
    shards = [shard]
    for step in range(1, size):
        far = shift(piece, size, size - step)
        shards.append(lax.all_gather(far, "dp", axis=dim, tiled=True))
    return shards


def scatter_blocks(make, dp_size, dp_rank):
    bits = dp_size.bit_length() - 1
    core = dp_rank % 2
    evens = 2 * jnp.arange(dp_size // 2)
    away = swap(make(evens + (1 - core)).astype(BF16), dp_size, 0)
    near = make(evens + core) + away.astype(F32)
    half = near.shape[1] // 2
    done = []
    for part in range(2):
        total = near[:, part * half : (part + 1) * half]
        order = list(range(1, bits))
        if part == 1 and len(order) > 1:
            order[0], order[1] = order[1], order[0]
        left = list(range(1, bits))
        for bit in order:
            place = left.index(bit)
            shape = (2 ** (len(left) - 1 - place), 2, 2**place) + total.shape[1:]
            split = total.reshape(shape)
            mine = (dp_rank >> bit) & 1
            keep = lax.dynamic_index_in_dim(split, mine, 1, keepdims=False)
            send = lax.dynamic_index_in_dim(split, 1 - mine, 1, keepdims=False)
            got = swap(send.astype(BF16), dp_size, bit)
            total = (keep + got.astype(F32)).reshape((-1,) + total.shape[1:])
            left.remove(bit)
        done.append(total[0])
    return jnp.concatenate(done, axis=0)


def scatter_shards(partials, size):
    total = partials[0]
    for step in range(1, size):
        total = total + shift(partials[step].astype(BF16), size, step).astype(F32)
    return total


def turn(values_t, cosine, sine):
    half = HD // 2
    front, back = values_t[:, :half], values_t[:, half:]
    return jnp.concatenate([front * cosine - back * sine, back * cosine + front * sine], axis=1)


def rolled(parts, rank):
    size = len(parts)
    both = jnp.concatenate(parts + parts[: size - 1], axis=0)
    length = parts[0].shape[0]
    return lax.dynamic_slice_in_dim(both, lax.rem(size - rank, size) * length, size * length, 0)


def local(
    layer_input, positions, norm_first, w_query, w_key, w_value, w_out, norm_second, w_gate, w_up, w_down, cotangent
):
    size = lax.axis_size("tensor")
    rank = lax.axis_index("tensor")
    dp_size = lax.axis_size("dp")
    dp_rank = lax.axis_index("dp")
    capacity = layer_input.shape[0]
    width = w_key.shape[0]
    kv = w_key.shape[1] // HD
    rows = capacity // size
    block = rows // NB
    heads = w_query.shape[1] * size // HD
    hidden = w_gate.shape[1]

    gain_first = lax.all_gather(norm_first, "tensor", axis=0, tiled=True).astype(F32)
    gain_second = lax.all_gather(norm_second, "tensor", axis=0, tiled=True).astype(F32)

    x_low = to_rows(layer_input, size, rank)
    own_ids = jnp.stack([r * size + (rank if r % 2 == 0 else size - 1 - rank) for r in range(NB)])
    place_blocks = positions.reshape(NB * size, block)
    own_places = jnp.concatenate([pick(place_blocks, own_ids[r])[None] for r in range(NB)], axis=0)
    own_index = own_ids[:, None] * block + jnp.arange(block, dtype=jnp.int32)[None, :]
    lows = own_index - jnp.maximum(own_places, 0)
    most, least = jnp.max(lows, axis=1), jnp.min(lows, axis=1)
    last = (own_ids * block + block + KC - 1) // KC
    first = least // KC
    full_first = jnp.minimum((most + KC - 1) // KC, last)
    full_last = jnp.clip((own_ids * block + 1) // KC, full_first, last)
    bounds = jnp.stack([first, full_first, full_last, last], axis=1).astype(jnp.int32)
    lows = lows[:, None, :]
    highs = own_index[:, None, :]

    frequency = 10000.0 ** (-(jnp.arange(HD // 2, dtype=F32) * 2.0 / HD))
    angles = own_places.reshape(1, rows).astype(F32) * frequency[:, None]
    cosine, sine = jnp.cos(angles), jnp.sin(angles)

    query_w = gather_shards(w_query, 0, dp_size, dp_rank, size)
    out_w = gather_shards(w_out, 0, dp_size, dp_rank, size)
    gate_up = jnp.concatenate([w_gate, w_up], axis=1)
    gate_up_w = gather_shards(gate_up, 0, dp_size, dp_rank, size)
    down_w = gather_shards(w_down, 0, dp_size, dp_rank, size)

    x_rows = x_low.astype(F32)
    scale_first = lax.rsqrt(jnp.mean(x_rows * x_rows, axis=1, keepdims=True) + EPS)
    xn1 = (x_rows * scale_first * gain_first).astype(BF16)
    key_t = mm(w_key, xn1, ((0,), (1,)))
    key_rows = turn(key_t.reshape(kv, HD, rows), cosine, sine).reshape(kv * HD, rows).astype(BF16).T
    value_rows = mm(xn1, w_value, ((1,), (0,))).astype(BF16)
    own_kv = jnp.concatenate([key_rows, value_rows], axis=1)
    all_kv = by_place(
        jnp.stack([own_kv] * size) if size == 1 else lax.all_gather(own_kv, "tensor", axis=0, tiled=False)
    )
    keys = all_kv[:, : kv * HD].reshape(capacity, kv, HD).transpose(1, 0, 2)
    values = all_kv[:, kv * HD :].reshape(capacity, kv, HD).transpose(1, 0, 2)

    def chunked_t(array):
        return array.reshape(kv, capacity // KC, KC, HD).transpose(0, 1, 3, 2)

    keys_t = chunked_t(keys)
    ones = jnp.ones((kv, capacity // KC, SUM_ROWS, KC), BF16)
    values_t = jnp.concatenate([chunked_t(values), ones], axis=2)

    def to_blocks(array_t):
        return array_t.reshape(array_t.shape[0], NB, block).transpose(1, 0, 2)

    def from_blocks(blocks_t):
        return blocks_t.transpose(1, 0, 2).reshape(blocks_t.shape[1], rows)

    q_lin_t = rolled([mm(w, xn1, ((0,), (1,))) for w in query_w], rank)
    q_t = (turn(q_lin_t.reshape(heads, HD, rows), cosine, sine) * 0.125).reshape(heads * HD, rows).astype(BF16)
    q_t = to_blocks(q_t)
    o_blocks, lse = attend(bounds, q_t, lows, highs, keys, values_t)
    o_t = from_blocks(o_blocks)
    own_slab = heads * HD // size
    o_parts = [
        lax.dynamic_slice_in_dim(o_t, lax.rem(rank + k, size) * own_slab, own_slab, 0) for k in range(size)
    ]
    h = x_rows
    for k in range(size):
        h = h + mm(o_parts[k], out_w[k], ((0,), (0,)))

    scale_second = lax.rsqrt(jnp.mean(h * h, axis=1, keepdims=True) + EPS)
    xn2 = (h * scale_second * gain_second).astype(BF16)
    y = to_rows(cotangent, size, rank)
    result = h
    a_parts, gu_parts = [], []
    for k in range(size):
        gate_act_up = mm(xn2, gate_up_w[k], ((1,), (0,)))
        gate_act, upward = gate_act_up[:, :hidden], gate_act_up[:, hidden:]
        a_parts.append((gate_act * jax.nn.sigmoid(gate_act) * upward).astype(BF16))
        gu_parts.append(gate_act_up.astype(BF16))
    for k in range(size):
        result = result + mm(a_parts[k], down_w[k], ((1,), (0,)))
    mixed = to_features(result.astype(BF16), size, rank)

    def split_cols(array):
        return array.reshape(rows, dp_size, width // dp_size).transpose(1, 0, 2)

    def block_rows(source, other):
        stacks = split_cols(source)

        def make(index):
            chosen = stacks[index]
            return lax.dot_general(chosen, other, (((1,), (0,)), ((), ())), preferred_element_type=F32)

        return make

    d_parts = []
    for k in range(size):
        da = mm(y, down_w[k], ((1,), (1,)))
        gate_act = gu_parts[k][:, :hidden].astype(F32)
        upward = gu_parts[k][:, hidden:].astype(F32)
        sig = jax.nn.sigmoid(gate_act)
        d_gate = (da * upward * sig * (1.0 + gate_act * (1.0 - sig))).astype(BF16)
        d_up = (da * gate_act * sig).astype(BF16)
        d_parts.append(jnp.concatenate([d_gate, d_up], axis=1))
    grad_down = scatter_shards([scatter_blocks(block_rows(y, a), dp_size, dp_rank) for a in a_parts], size).T
    dxn2 = jnp.zeros((rows, width), F32)
    for k in range(size):
        dxn2 = dxn2 + mm(d_parts[k], gate_up_w[k], ((1,), (1,)))
    grad_gate_up = scatter_shards([scatter_blocks(block_rows(xn2, d), dp_size, dp_rank) for d in d_parts], size)
    scaled = dxn2 * gain_second
    stat_second = jnp.sum(scaled * h, axis=1, keepdims=True)
    dh = y.astype(F32) + scaled * scale_second - h * (scale_second**3 * stat_second / width)
    gain_two = jnp.sum(dxn2 * h * scale_second, axis=0)
    dhb = dh.astype(BF16)

    do_t = to_blocks(rolled([mm(w, dhb, ((1,), (1,))).astype(BF16) for w in out_w], rank))
    dq_blocks, d_keys, d_values = attend_back(bounds, q_t, do_t, o_blocks, lse, lows, highs, keys, values, keys_t)

    def block_rows_t(source, other_t):
        stacks = split_cols(source)

        def make(index):
            chosen = stacks[index]
            return lax.dot_general(chosen, other_t, (((1,), (1,)), ((), ())), preferred_element_type=F32)

        return make

    grad_out = scatter_shards([scatter_blocks(block_rows_t(dhb, o), dp_size, dp_rank) for o in o_parts], size).T
    d_kv = jnp.concatenate(
        [
            d_keys.transpose(1, 0, 2).reshape(capacity, kv * HD),
            d_values.transpose(1, 0, 2).reshape(capacity, kv * HD),
        ],
        axis=1,
    ).astype(BF16)
    own_dkv = jnp.sum(exchange(by_owner(d_kv, size), rank).astype(F32), axis=0)
    dk_lin = (
        turn(own_dkv[:, : kv * HD].T.reshape(kv, HD, rows), cosine, -sine).reshape(kv * HD, rows).T.astype(BF16)
    )
    dv_lin = own_dkv[:, kv * HD :].astype(BF16)
    dq_t = from_blocks(dq_blocks).reshape(heads, HD, rows) * 0.125
    dq_t = turn(dq_t, cosine, -sine).reshape(heads * HD, rows).astype(BF16)
    dq_parts = [
        lax.dynamic_slice_in_dim(dq_t, lax.rem(rank + k, size) * own_slab, own_slab, 0) for k in range(size)
    ]
    dxn1 = mm(dk_lin, w_key, ((1,), (1,))) + mm(dv_lin, w_value, ((1,), (1,)))
    for k in range(size):
        dxn1 = dxn1 + mm(dq_parts[k], query_w[k], ((0,), (1,)))
    scaled = dxn1 * gain_first
    stat_first = jnp.sum(scaled * x_rows, axis=1, keepdims=True)
    dx = dh + scaled * scale_first - x_rows * (scale_first**3 * stat_first / width)
    grad_input = to_features(dx.astype(BF16), size, rank).astype(F32)
    gain_one = jnp.sum(dxn1 * x_rows * scale_first, axis=0)

    grad_query = scatter_shards([scatter_blocks(block_rows_t(xn1, d), dp_size, dp_rank) for d in dq_parts], size)
    kv_block = scatter_blocks(block_rows(xn1, jnp.concatenate([dk_lin, dv_lin], axis=1)), dp_size, dp_rank)
    kv_stack = kv_block.astype(BF16).reshape(size, kv_block.shape[0] // size, kv_block.shape[1])
    grad_kv = jnp.sum(exchange(kv_stack, rank).astype(F32), axis=0)
    gains = lax.psum_scatter(jnp.stack([gain_one, gain_two], axis=1), ("dp", "tensor"), scatter_dimension=0, tiled=True)

    return (
        mixed,
        grad_input,
        gains[:, 0],
        grad_query,
        grad_kv[:, : kv * HD],
        grad_kv[:, kv * HD :],
        grad_out,
        gains[:, 1],
        grad_gate_up[:, :hidden],
        grad_gate_up[:, hidden:],
        grad_down,
    )


def solution(mesh):
    return jax.shard_map(
        local,
        mesh=mesh,
        in_specs=(
            P("dp", "tensor"),
            P("dp"),
            P("tensor"),
            P(None, "tensor"),
            P(),
            P(),
            P("tensor", None),
            P("tensor"),
            P(None, "tensor"),
            P(None, "tensor"),
            P("tensor", None),
            P("dp", "tensor"),
        ),
        out_specs=(
            P("dp", "tensor"),
            P("dp", "tensor"),
            P(("dp", "tensor")),
            P("dp", "tensor"),
            P(("dp", "tensor"), None),
            P(("dp", "tensor"), None),
            P("tensor", "dp"),
            P(("dp", "tensor")),
            P("dp", "tensor"),
            P("dp", "tensor"),
            P("tensor", "dp"),
        ),
        check_vma=False,
    )
```

time: 2360 us -> 2310 us (0.979); the launches traced: 2360 us -> 2270 us
  waiting for transfers between devices: 1330 us -> 835 us
  local copies, waits for them, and re-layouts: 47 us -> 462 us
  starting transfers between devices: 0.62 us -> 262 us
  matrix products: 638 us -> 413 us
  other arithmetic: 220 us -> 76.9 us
  Pallas kernels: 0 us -> 114 us
    reduce_scatter x11 -> x0, waiting for transfers between devices: 755 us -> none  [the longest x1 182 us: local(): lax.psum_scatter(grad_normed_first.astype(jnp.bfloat16), 'tensor', scatte...]
    ppermute x0 -> x127, waiting for transfers between devices: none -> 685 us  [the longest x42 430 us: shift(): lax.ppermute(array, 'tensor', [(i, (i + step) % size) for i in range(size)])]
    all_gather x4 -> x13, waiting for transfers between devices: 574 us -> 0.04 us  [the longest x12 0.04 us: gather_shards(): shards.append(lax.all_gather(far, 'dp', axis=dim, tiled=True))]
    ppermute x0 -> x127, starting transfers between devices: none -> 261 us  [the longest x85 162 us: swap(): return lax.ppermute(array, 'dp', [(i, i ^ 1 << bit) for i in range(size)])]
    dot_general x51 -> x70, matrix products: 638 us -> 413 us  [the longest x36 275 us: mm(): lax.dot_general(left, right, ((dims[0], dims[1]), ((), ())), preferred_el...]
    unnamed x15, waiting for transfers between devices: 1.42 us -> 150 us
    pallas_call x0 -> x2, Pallas kernels: none -> 114 us  [the longest x1 58.2 us: attend(): pl.pallas_call(forward_kernel, out_shape=(jax.ShapeDtypeStruct((blocks, w...]
    unnamed x251 -> x578, local copies, waits for them, and re-layouts: 27.1 us -> 129 us
  transfers between devices with their start and end apart: 15 -> 141, of which waited for: 10 -> 66; matrix products, arithmetic and copies ran while one was open for 25% -> 33% of each run, Pallas kernels for 0% -> 3%
where the time goes in v1:
time: 2310 us; the launch traced here: 2270 us
  waiting for transfers between devices  835 us (36%)
  local copies, waits for them, and re-layouts  462 us (20%)
  matrix products  413 us (18%)
  starting transfers between devices  262 us (11%)
  Pallas kernels  114 us (5%)
  blocking collectives  90.3 us (4%)
  other arithmetic  76.9 us (3%)
    ppermute x42, waiting for transfers between devices, shift(): lax.ppermute(array, 'tensor', [(i, (i + step) % size) for i in range(size)])  430 us
    dot_general x36, matrix products, mm(): lax.dot_general(left, right, ((dims[0], dims[1]), ((), ())), preferred_el...  275 us
    ppermute x85, waiting for transfers between devices, swap(): return lax.ppermute(array, 'dp', [(i, i ^ 1 << bit) for i in range(size)])  255 us
    ppermute x85, starting transfers between devices, swap(): return lax.ppermute(array, 'dp', [(i, i ^ 1 << bit) for i in range(size)])  162 us
    unnamed x15, waiting for transfers between devices  150 us
    unnamed x578, local copies, waits for them, and re-layouts  129 us
    dot_general x18, matrix products, make(): lax.dot_general(chosen, other, (((1,), (0,)), ((), ())), preferred_elemen...  106 us
    ppermute x42, starting transfers between devices, shift(): lax.ppermute(array, 'tensor', [(i, (i + step) % size) for i in range(size)])  99.2 us
  transfers between devices with their start and end apart: 141, of which 66 were waited for; matrix products, arithmetic and copies ran while one was open for 33% of the time, Pallas kernels for 3%

profile of v1, /device:TPU:0, one launch (start us, length us, event | category | flops | bytes accessed | tf_op | source)
XLA Modules:
  0.0 2271.7 jit_solution(13466484190092489323)
XLA Ops:
  53.4 67.4 %all-gather.1 = bf16[4,1,512]{2,1,0:T(2,128)(2,1)S(1)} all-gather(bf16[1,1,512]{2,1,0:T(2,128)(2,1)S(1)} %reshape.1749), channel_id=1, replica_groups=mesh['dp'=8,'tensor'=4] {'tensor'}, dimensions={0}, use_global_device_ids=true | all-gather | bytes 5120 | tf_op jit(solution)/shard_map/all_gather | solution.py:348
  126.6 23.9 %collective-permute-done = bf16[640,512]{1,0:T(8,128)(2,1)S(1)} collective-permute-done((bf16[640,512]{1,0:T(8,128)(2,1)}, bf16[640,512]{1,0:T(8,128)(2,1)S(1)}, u32[]{:S(2)}, u32[]{:S(2)}) %collective-permute-start) | collective-permute-done | bytes 655392 | tf_op jit(solution)/shard_map/ppermute | solution.py:229
  180.4 14.9 collective-permute-start.6
  203.2 30.1 %collective-permute-done.7 = bf16[64,2048]{1,0:T(8,128)(2,1)S(1)} collective-permute-done((bf16[64,2048]{1,0:T(8,128)(2,1)S(1)}, bf16[64,2048]{1,0:T(8,128)(2,1)S(1)}, u32[]{:S(2)}, u32[]{:S(2)}) %collective-permute-start.7) | collective-permute-done | bytes 262176 | tf_op jit(solution)/shard_map/ppermute | solution.py:229
  234.2 16.0 collective-permute-done.8
  264.7 31.3 %collective-permute-done.9 = bf16[256,2816]{1,0:T(8,128)(2,1)} collective-permute-done((bf16[256,2816]{1,0:T(8,128)(2,1)S(1)}, bf16[256,2816]{1,0:T(8,128)(2,1)}, u32[]{:S(2)}, u32[]{:S(2)}) %collective-permute-start.9) | collective-permute-done | bytes 1441824 | tf_op jit(solution)/shard_map/ppermute | solution.py:229
  318.1 62.0 %collective-permute-done.11 = bf16[256,2816]{1,0:T(8,128)(2,1)} collective-permute-done((bf16[256,2816]{1,0:T(8,128)(2,1)}, bf16[256,2816]{1,0:T(8,128)(2,1)}, u32[]{:S(2)}, u32[]{:S(2)}) %collective-permute-start.11) | collective-permute-done | bytes 1441824 | tf_op jit(solution)/shard_map/ppermute | solution.py:229
  380.2 32.9 %collective-permute-done.12 = bf16[176,2048]{1,0:T(8,128)(2,1)S(1)} collective-permute-done((bf16[176,2048]{1,0:T(8,128)(2,1)}, bf16[176,2048]{1,0:T(8,128)(2,1)S(1)}, u32[]{:S(2)}, u32[]{:S(2)}) %collective-permute-start.12) | collective-permute-done | bytes 720928 | tf_op jit(solution)/shard_map/ppermute | solution.py:229
  414.1 34.0 %collective-permute-done.13 = bf16[256,2816]{1,0:T(8,128)(2,1)} collective-permute-done((bf16[256,2816]{1,0:T(8,128)(2,1)}, bf16[256,2816]{1,0:T(8,128)(2,1)}, u32[]{:S(2)}, u32[]{:S(2)}) %collective-permute-start.13) | collective-permute-done | bytes 1441824 | tf_op jit(solution)/shard_map/ppermute | solution.py:229
  448.9 22.9 %all-gather.2 = bf16[4,1,512]{2,1,0:T(2,128)(2,1)S(1)} all-gather(bf16[1,1,512]{2,1,0:T(2,128)(2,1)S(1)} %reshape.1751), channel_id=1, replica_groups=mesh['dp'=8,'tensor'=4] {'tensor'}, dimensions={0}, use_global_device_ids=true | all-gather | bytes 5120 | tf_op jit(solution)/shard_map/all_gather | solution.py:349
  586.8 58.2 %attention_forward.1 = (bf16[5,2048,128]{2,1,0:T(8,128)(2,1)S(1)}, f32[5,4,8,128]{3,2,1,0:T(8,128)S(1)}) custom-call(s32[5,4]{1,0:T(8,128)S(1)} %pad_add_fusion.bounds_ref, bf16[5,2048,128]{2,1,0:T(8,128)(2,1)S(1)} %bitcast.852, s32[5,1,128]{2,1,0:T(1,128)S(1)} %get-tuple-element.154.lo_ref, s32[5,1,128]{2,1,0:T(1,128)S(1)} %get-tuple-element.153.hi_ref, ...), custom_call_target="tpu_custom_call" | custom-call | flops 26843545600 | bytes 12582912 | tf_op jit(solution)/shard_map/attention_forward/pallas_call | solution.py:158
  707.0 28.0 %collective-permute-start.104 = (bf16[4,256,1408]{2,1,0:T(8,128)(2,1)}, bf16[4,256,1408]{2,1,0:T(8,128)(2,1)}, u32[]{:S(2)}, u32[]{:S(2)}) collective-permute-start(bf16[4,256,1408]{2,1,0:T(8,128)(2,1)} %convolution_convert_fusion.7), channel_id=1, source_target_pairs={{0,4},{4,0},{8,12},{12,8},{16,20},{20,16},{24,28},{28,24},{1,5},{5... | collective-permute-start | bytes 8650760 | tf_op jit(solution)/shard_map/ppermute | solution.py:233
  806.0 32.0 %collective-permute-start.107 = (bf16[1,2,128,1408]{2,3,1,0:T(8,128)(2,1)}, bf16[1,2,128,1408]{2,3,1,0:T(8,128)(2,1)S(1)}, u32[]{:S(2)}, u32[]{:S(2)}) collective-permute-start(bf16[1,2,128,1408]{2,3,1,0:T(8,128)(2,1)} %bitcast.1043), channel_id=1, source_target_pairs={{0,16},{4,20},{8,24},{12,28},{16,0},{20,4},{24,8},{28,12},{1,17},{... | collective-permute-start | bytes 2162696 | tf_op jit(solution)/shard_map/ppermute | solution.py:233
  882.6 33.5 %collective-permute-done.108 = bf16[1,1,128,1408]{2,3,1,0:T(8,128)(2,1)S(1)} collective-permute-done((bf16[1,1,128,1408]{2,3,1,0:T(8,128)(2,1)S(1)}, bf16[1,1,128,1408]{2,3,1,0:T(8,128)(2,1)S(1)}, u32[]{:S(2)}, u32[]{:S(2)}) %collective-permute-start.108) | collective-permute-done | bytes 360480 | tf_op jit(solution)/shard_map/ppermute | solution.py:233
  935.9 14.9 fusion.318
  1002.4 14.8 fusion.319
  1058.7 17.9 multiply_reduce_fusion
  1126.1 55.6 %attention_backward.1 = (f32[5,2048,128]{2,1,0:T(8,128)S(1)}, f32[4,2560,64]{2,1,0:T(8,128)}, f32[4,2560,64]{2,1,0:T(8,128)}) custom-call(s32[5,4]{1,0:T(8,128)S(1)} %copy-done.11, bf16[5,2048,128]{2,1,0:T(8,128)(2,1)S(1)} %bitcast.853, bf16[5,2048,128]{2,1,0:T(8,128)(2,1)S(1)} %bitcast.855, bf16[5,2048,128]{2,1,0:T(8,128)(2,1)S(1)} %copy-done.6, ...), custom_call_target="tpu_custom_call" | custom-call | flops 67108864000 | bytes 25165824 | tf_op jit(solution)/shard_map/attention_backward/pallas_call | solution.py:198
  1225.0 26.5 %collective-permute-start.109 = (bf16[4,256,1408]{2,1,0:T(8,128)(2,1)}, bf16[4,256,1408]{2,1,0:T(8,128)(2,1)}, u32[]{:S(2)}, u32[]{:S(2)}) collective-permute-start(bf16[4,256,1408]{2,1,0:T(8,128)(2,1)} %convolution_convert_fusion.6), channel_id=1, source_target_pairs={{0,4},{4,0},{8,12},{12,8},{16,20},{20,16},{24,28},{28,24},{1,5},{5... | collective-permute-start | bytes 8650760 | tf_op jit(solution)/shard_map/ppermute | solution.py:233
  1359.9 19.4 subtract_convert_fusion
  1417.0 150.1 %reduce-scatter.4.cloned.1.call-done = f32[64,2]{1,0:T(8,128)} async-done(((f32[2048,2]{1,0:T(8,128)}), f32[64,2]{1,0:T(8,128)}) %reduce-scatter.4.cloned.1.call-update) | async-done | bytes 528
  1688.3 29.3 %collective-permute-done.16 = bf16[640,512]{1,0:T(8,128)(2,1)S(1)} collective-permute-done((bf16[640,512]{1,0:T(8,128)(2,1)S(1)}, bf16[640,512]{1,0:T(8,128)(2,1)S(1)}, u32[]{:S(2)}, u32[]{:S(2)}) %collective-permute-start.16) | collective-permute-done | bytes 655392 | tf_op jit(solution)/shard_map/ppermute | solution.py:229
  2107.0 18.0 collective-permute-done.101
  2173.8 86.1 %collective-permute-done.126 = bf16[256,1408]{0,1:T(8,128)(2,1)S(1)} collective-permute-done((bf16[256,1408]{0,1:T(8,128)(2,1)S(1)}, bf16[256,1408]{0,1:T(8,128)(2,1)S(1)}, u32[]{:S(2)}, u32[]{:S(2)}) %collective-permute-start.126) | collective-permute-done | bytes 720928 | tf_op jit(solution)/shard_map/ppermute | solution.py:229
  (1271 shorter events, 1333.8 us)
Async XLA Ops:
  7.2 513.0 %all-gather.17.cloned.1.call-start = ((), (), s32[]{:S(2)}) async-start(), calls=%async_computation.1 | async-start | bytes 2359296 | tf_op jit(solution)/shard_map/all_gather | solution.py:281
  20.7 505.2 %all-gather.19.cloned.1.call-start = ((), (), s32[]{:S(2)}) async-start(), calls=%async_computation.2 | async-start | bytes 2359296 | tf_op jit(solution)/shard_map/all_gather | solution.py:281
  35.5 496.2 %all-gather.21.cloned.1.call-start = ((), (), s32[]{:S(2)}) async-start(), calls=%async_computation.3 | async-start | bytes 2359296 | tf_op jit(solution)/shard_map/all_gather | solution.py:281
  121.9 436.4 %all-gather.41.cloned.1.call-start = ((), (), s32[]{:S(2)}) async-start(), calls=%async_computation.13 | async-start | bytes 3276800 | tf_op jit(solution)/shard_map/all_gather | solution.py:384
  180.3 475.8 %all-gather.23.cloned.1.call-start = ((), (), s32[]{:S(2)}) async-start(), calls=%async_computation.4 | async-start | bytes 2359296 | tf_op jit(solution)/shard_map/all_gather | solution.py:281
  202.1 459.5 %all-gather.25.cloned.1.call-start = ((), (), s32[]{:S(2)}) async-start(), calls=%async_computation.5 | async-start | bytes 2359296 | tf_op jit(solution)/shard_map/all_gather | solution.py:281
  234.1 433.5 %all-gather.27.cloned.1.call-start = ((), (), s32[]{:S(2)}) async-start(), calls=%async_computation.6 | async-start | bytes 2359296 | tf_op jit(solution)/shard_map/all_gather | solution.py:281
  250.9 685.0 %all-gather.29.cloned.1.call-start = ((), (), s32[]{:S(2)}) async-start(), calls=%async_computation.7 | async-start | bytes 12976128 | tf_op jit(solution)/shard_map/all_gather | solution.py:281
  295.9 654.8 %all-gather.31.cloned.1.call-start = ((), (), s32[]{:S(2)}) async-start(), calls=%async_computation.8 | async-start | bytes 6488064 | tf_op jit(solution)/shard_map/all_gather | solution.py:281
  316.7 652.5 %all-gather.33.cloned.1.call-start = ((), (), s32[]{:S(2)}) async-start(), calls=%async_computation.9 | async-start | bytes 12976128 | tf_op jit(solution)/shard_map/all_gather | solution.py:281
  380.1 603.9 %all-gather.35.cloned.1.call-start = ((), (), s32[]{:S(2)}) async-start(), calls=%async_computation.10 | async-start | bytes 6488064 | tf_op jit(solution)/shard_map/all_gather | solution.py:281
  414.0 588.4 %all-gather.37.cloned.1.call-start = ((), (), s32[]{:S(2)}) async-start(), calls=%async_computation.11 | async-start | bytes 12976128 | tf_op jit(solution)/shard_map/all_gather | solution.py:281
  448.1 569.1 %all-gather.39.cloned.1.call-start = ((), (), s32[]{:S(2)}) async-start(), calls=%async_computation.12 | async-start | bytes 6488064 | tf_op jit(solution)/shard_map/all_gather | solution.py:281
  520.1 1047.0 %reduce-scatter.4.cloned.1.call-start = ((), (), s32[]{:S(2)}) async-start(), calls=%async_computation.14 | async-start | bytes 1081344
  1225.0 637.4 %collective-permute-start.109 = (bf16[4,256,1408]{2,1,0:T(8,128)(2,1)}, bf16[4,256,1408]{2,1,0:T(8,128)(2,1)}, u32[]{:S(2)}, u32[]{:S(2)}) collective-permute-start(bf16[4,256,1408]{2,1,0:T(8,128)(2,1)} %convolution_convert_fusion.6), channel_id=1, source_target_pairs={{0,4},{4,0},{8,12},{12,8},{16,20},{20,16},{24,28},{28,24},{1,5},{5... | collective-permute-start | bytes 8650760 | tf_op jit(solution)/shard_map/ppermute | solution.py:233
  1261.8 307.4 %collective-permute-start.75 = (bf16[4,256,512]{2,1,0:T(8,128)(2,1)}, bf16[4,256,512]{2,1,0:T(8,128)(2,1)}, u32[]{:S(2)}, u32[]{:S(2)}) collective-permute-start(bf16[4,256,512]{2,1,0:T(8,128)(2,1)} %convolution_convert_fusion.8), channel_id=1, source_target_pairs={{0,4},{4,0},{8,12},{12,8},{16,20},{20,16},{24,28},{28,24},{1,5},{5... | collective-permute-start | bytes 3145736 | tf_op jit(solution)/shard_map/ppermute | solution.py:233
  1325.2 247.4 %collective-permute-start.58 = (bf16[4,256,512]{2,1,0:T(8,128)(2,1)}, bf16[4,256,512]{2,1,0:T(8,128)(2,1)}, u32[]{:S(2)}, u32[]{:S(2)}) collective-permute-start(bf16[4,256,512]{2,1,0:T(8,128)(2,1)} %convolution_convert_fusion.11), channel_id=1, source_target_pairs={{0,4},{4,0},{8,12},{12,8},{16,20},{20,16},{24,28},{28,24},{1,5},{5... | collective-permute-start | bytes 3145736 | tf_op jit(solution)/shard_map/ppermute | solution.py:233
  1335.6 242.8 %collective-permute-start.63 = (bf16[4,256,512]{2,1,0:T(8,128)(2,1)}, bf16[4,256,512]{2,1,0:T(8,128)(2,1)}, u32[]{:S(2)}, u32[]{:S(2)}) collective-permute-start(bf16[4,256,512]{2,1,0:T(8,128)(2,1)} %convolution_convert_fusion.10), channel_id=1, source_target_pairs={{0,4},{4,0},{8,12},{12,8},{16,20},{20,16},{24,28},{28,24},{1,5},{5... | collective-permute-start | bytes 3145736 | tf_op jit(solution)/shard_map/ppermute | solution.py:233
  1335.7 246.5 %collective-permute-start.69 = (bf16[4,256,512]{2,1,0:T(8,128)(2,1)}, bf16[4,256,512]{2,1,0:T(8,128)(2,1)}, u32[]{:S(2)}, u32[]{:S(2)}) collective-permute-start(bf16[4,256,512]{2,1,0:T(8,128)(2,1)} %convolution_convert_fusion.9), channel_id=1, source_target_pairs={{0,4},{4,0},{8,12},{12,8},{16,20},{20,16},{24,28},{28,24},{1,5},{5... | collective-permute-start | bytes 3145736 | tf_op jit(solution)/shard_map/ppermute | solution.py:233
  1587.2 207.6 %collective-permute-start.50 = (bf16[4,256,512]{2,1,0:T(8,128)(2,1)}, bf16[4,256,512]{2,1,0:T(8,128)(2,1)}, u32[]{:S(2)}, u32[]{:S(2)}) collective-permute-start(bf16[4,256,512]{2,1,0:T(8,128)(2,1)} %convolution_convert_fusion.12), channel_id=1, source_target_pairs={{0,4},{4,0},{8,12},{12,8},{16,20},{20,16},{24,28},{28,24},{1,5},{5... | collective-permute-start | bytes 3145736 | tf_op jit(solution)/shard_map/ppermute | solution.py:233
  1801.8 188.6 %collective-permute-start.86 = (bf16[4,256,2816]{2,1,0:T(8,128)(2,1)}, bf16[4,256,2816]{2,1,0:T(8,128)(2,1)}, u32[]{:S(2)}, u32[]{:S(2)}) collective-permute-start(bf16[4,256,2816]{2,1,0:T(8,128)(2,1)} %convolution_convert_fusion.2), channel_id=1, source_target_pairs={{0,4},{4,0},{8,12},{12,8},{16,20},{20,16},{24,28},{28,24},{1,5},{5... | collective-permute-start | bytes 17301512 | tf_op jit(solution)/shard_map/ppermute | solution.py:233
  1839.9 174.4 %collective-permute-start.92 = (bf16[4,256,2816]{2,1,0:T(8,128)(2,1)}, bf16[4,256,2816]{2,1,0:T(8,128)(2,1)}, u32[]{:S(2)}, u32[]{:S(2)}) collective-permute-start(bf16[4,256,2816]{2,1,0:T(8,128)(2,1)} %convolution_convert_fusion.1), channel_id=1, source_target_pairs={{0,4},{4,0},{8,12},{12,8},{16,20},{20,16},{24,28},{28,24},{1,5},{5... | collective-permute-start | bytes 17301512 | tf_op jit(solution)/shard_map/ppermute | solution.py:233
  1988.7 184.2 %collective-permute-start.114 = (bf16[256,1408]{0,1:T(8,128)(2,1)}, bf16[256,1408]{0,1:T(8,128)(2,1)}, u32[]{:S(2)}, u32[]{:S(2)}) collective-permute-start(bf16[256,1408]{0,1:T(8,128)(2,1)} %pad_maximum_fusion.22), channel_id=1, source_target_pairs={{0,1},{1,2},{2,3},{3,0},{4,5},{5,6},{6,7},{7,4},{8,9},{9,10},{10,1... | collective-permute-start | bytes 2162696 | tf_op jit(solution)/shard_map/ppermute | solution.py:229
  1990.3 183.4 %collective-permute-start.120 = (bf16[256,1408]{0,1:T(8,128)(2,1)}, bf16[256,1408]{0,1:T(8,128)(2,1)}, u32[]{:S(2)}, u32[]{:S(2)}) collective-permute-start(bf16[256,1408]{0,1:T(8,128)(2,1)} %pad_maximum_fusion.23), channel_id=1, source_target_pairs={{0,2},{1,3},{2,0},{3,1},{4,6},{5,7},{6,4},{7,5},{8,10},{9,11},{10,... | collective-permute-start | bytes 2162696 | tf_op jit(solution)/shard_map/ppermute | solution.py:229
  (359 other events, 8216.7 us)
Sparse Core Ops, SparseCore 0:
  20.8 29.7 all-gather.16
  52.5 27.9 all-gather.18
  122.1 28.4 all-gather.20
  180.4 83.8 all-gather.40
  266.1 26.4 all-gather.22
  294.3 27.8 all-gather.24
  324.7 27.8 all-gather.26
  354.5 67.6 all-gather.28
  424.1 43.3 all-gather.30
  469.2 67.6 all-gather.32
  538.8 43.3 all-gather.34
  583.9 67.8 all-gather.36
  653.7 43.3 all-gather.38
  1386.4 180.6 reduce-scatter.3
